TPU v7x, 512 devices: a whole 4x8x8 slice. The times are simulated.
512 devices in a mesh: section: 16 (over y, z_hi), dp: 16 (over z_lo, x), cores: 2 (over core).
Axes of the slice: x: 4, y: 8, z: 8 (z_hi: 2, z_lo: 4; z = z_hi * 4 + z_lo), core: 2. Of those that a mesh axis runs over, the one named last changes fastest.
Arguments:
- arrivals: bfloat16 [2, 1536, 2048], P(None, 'dp'), may hold values from -6 to 6
- in_flight: bfloat16 [16, 1536, 2048], P('section', 'dp'), may hold values from -6 to 6
- cotangent: bfloat16 [2, 1536, 2048], P(None, 'dp'), may hold values from -6 to 6
- grad_flight: bfloat16 [16, 1536, 2048], P('section', 'dp'), may hold values from -6 to 6
- stashed: bfloat16 [16, 2, 1536, 2048], P('section', None, 'dp'), may hold values from -6 to 6
- in_weight: bfloat16 [16, 2048, 4096], P('section', 'dp', 'cores'), may hold values from -0.125 to 0.125
- out_weight: bfloat16 [16, 1024, 2048], P('section', 'cores', 'dp'), may hold values from -0.1875 to 0.1875
- forward_blocks: int32 [16, 17], P('dp'), may hold values from 1 to 4, 42 in all within a row
- backward_blocks: int32 [16, 17], P('dp'), may hold values from 1 to 4, 42 in all within a row
- forward_marks: int32 [16, 17, 4, 4], P('dp'), may hold values 0 or 1
- backward_marks: int32 [16, 17, 4, 4], P('dp'), may hold values 0 or 1
Outputs:
- activations: bfloat16 [16, 2, 1536, 2048], P('section', None, ('dp', 'cores'))
- input_grads: bfloat16 [16, 2, 1536, 2048], P('section', None, ('dp', 'cores'))
- weight_grads: float32 [16, 1024, 2048], P('section', 'cores', 'dp')
Inputs may be any that keep to these rules, and one draw needn't show every extreme that they name: `forward_blocks`: in each replica's row the 17 lengths add up to 42 blocks and the longest is 4. `backward_blocks`: in each replica's row the 17 lengths add up to 42 blocks and the longest is 4.
All inputs are finite; a program needn't handle non-finite values. No bound on the sum of `forward_marks` or of `backward_marks` on one device may be relied on, other than what follows from the above.
Results may differ from a plain program's by a relative error of at most 0.03.
Values may be sent and summed in bfloat16 or wider, within the bound.
A program may use at most 64 MiB of HBM per device.

v0:
```python
import jax
import jax.numpy as jnp
from jax import lax
from jax.sharding import PartitionSpec as P

HEAD_DIM = 128
BLOCK = 24
BLOCKS = 4
EPSILON = 1e-06


def from_behind(x, axis, by):
    peers = lax.axis_size(axis)
    pairs = [(i, i + by) for i in range(peers) if 0 <= i + by < peers]
    return lax.ppermute(x, axis, pairs)


def block_keep(live_blocks, block_marks):
    length = BLOCKS * BLOCK
    places = jnp.arange(length, dtype=jnp.int32)
    owners = places // BLOCK
    onehot = (owners[:, None] == jnp.arange(BLOCKS, dtype=jnp.int32)[None, :]).astype(jnp.float32)
    spread = jnp.einsum("ia,rab,jb->rij", onehot, block_marks.astype(jnp.float32), onehot)
    allowed = (owners[:, None] == owners[None, :])[None] | (spread > 0.5)
    causal = (places[:, None] >= places[None, :])[None]
    tokens_live = live_blocks * BLOCK
    living = places[None, :] < tokens_live[:, None]
    keeping = causal & allowed & living[:, :, None] & living[:, None, :]
    return (keeping.astype(jnp.float32), 1.0 / tokens_live.astype(jnp.float32))


def choose_history(block_table, mark_table, history):
    histories = block_table.shape[1]
    matches = jnp.arange(histories, dtype=jnp.int32) == history
    blocks = jnp.sum(jnp.where(matches, block_table[0], 0))
    marked = jnp.sum(jnp.where(matches[:, None, None], mark_table[0], 0), axis=0)
    return block_keep(blocks[None], marked[None])


def norm_rows(values_f):
    return lax.rsqrt(jnp.mean(values_f * values_f, axis=-1, keepdims=True) + EPSILON)


def heads_forward(pre_act, keeping, inverse_count):
    scaling = HEAD_DIM ** (-0.5)
    active = jax.nn.silu(pre_act)
    gate_rows = active[:, :, :, 0]
    value_rows = active[:, :, :, 1].astype(jnp.bfloat16)
    query_rows = active[:, :, :, 2].astype(jnp.bfloat16)
    key_rows = active[:, :, :, 3].astype(jnp.bfloat16)
    scores = (
        jnp.einsum("rigd,rjgd->rgij", query_rows, key_rows, preferred_element_type=jnp.float32)
        * scaling
    )
    weights = keeping[:, None] * inverse_count[:, None, None, None]
    attention = (jax.nn.silu(scores) * weights).astype(jnp.bfloat16)
    mixed = jnp.einsum("rgij,rjgd->rigd", attention, value_rows, preferred_element_type=jnp.float32)
    root_scale = lax.rsqrt(jnp.mean(mixed * mixed, axis=-1, keepdims=True) + EPSILON)
    normed = mixed * root_scale
    gated = (normed * gate_rows).astype(jnp.bfloat16)
    return (
        gated,
        (
            gate_rows,
            value_rows,
            query_rows,
            key_rows,
            scores,
            weights,
            attention,
            root_scale,
            normed,
        ),
    )


def heads_backward(pre_act, saved, upstream):
    gate_rows, value_rows, query_rows, key_rows, scores, weights, attention, root_scale, normed = (
        saved
    )
    scaling = HEAD_DIM ** (-0.5)
    grad_gated = upstream.astype(jnp.float32)
    grad_normed = grad_gated * gate_rows
    grad_gate = grad_gated * normed
    grad_mixed = root_scale * (
        grad_normed - normed * jnp.mean(grad_normed * normed, axis=-1, keepdims=True)
    )
    mixed_low = grad_mixed.astype(jnp.bfloat16)
    grad_attention = jnp.einsum(
        "rigd,rjgd->rgij", mixed_low, value_rows, preferred_element_type=jnp.float32
    )
    grad_value = jnp.einsum(
        "rgij,rigd->rjgd", attention, mixed_low, preferred_element_type=jnp.float32
    )
    sigmoid_s = jax.nn.sigmoid(scores)
    grad_scores = (
        grad_attention * weights * sigmoid_s * (1.0 + scores * (1.0 - sigmoid_s)) * scaling
    ).astype(jnp.bfloat16)
    grad_query = jnp.einsum(
        "rgij,rjgd->rigd", grad_scores, key_rows, preferred_element_type=jnp.float32
    )
    grad_key = jnp.einsum(
        "rgij,rigd->rjgd", grad_scores, query_rows, preferred_element_type=jnp.float32
    )
    grad_active = jnp.stack([grad_gate, grad_value, grad_query, grad_key], axis=3)
    sigmoid_u = jax.nn.sigmoid(pre_act)
    return (grad_active * sigmoid_u * (1.0 + pre_act * (1.0 - sigmoid_u))).astype(jnp.bfloat16)


def per_device(
    arrivals,
    in_flight,
    cotangent,
    grad_flight,
    stashed,
    in_weight,
    out_weight,
    forward_blocks,
    backward_blocks,
    forward_marks,
    backward_marks,
):
    section_no = lax.axis_index("section")
    sections = lax.axis_size("section")
    core_no = lax.axis_index("cores")
    ticks = arrivals.shape[0]
    length = arrivals.shape[1]
    share = length // lax.axis_size("cores")
    row_start = core_no * share
    out_full = lax.all_gather(out_weight[0], "dp", axis=1, tiled=True)
    slab_rows = out_full.shape[0]
    groups = slab_rows // HEAD_DIM
    columns = in_weight.shape[2]
    in_full = None
    in_full = lax.all_gather(in_weight[0], "dp", axis=0, tiled=True)
    received = in_flight[0]
    returned = grad_flight[0]
    ahead_out = []
    back_out = []
    gated_list = []
    upstream_list = []
    for tick_no in range(ticks):
        if tick_no == 0:
            prior = in_flight[0]
            later = grad_flight[0]
        else:
            prior = received
            later = returned
        inputs = jnp.where(section_no == 0, arrivals[tick_no], prior)
        upstream = jnp.where(section_no == sections - 1, cotangent[tick_no], later)
        keep_ahead, count_ahead = choose_history(
            forward_blocks, forward_marks, tick_no - section_no + sections - 1
        )
        keep_back, count_back = choose_history(
            backward_blocks, backward_marks, tick_no + section_no
        )
        floats = inputs.astype(jnp.float32)
        saved_floats = stashed[0, tick_no].astype(jnp.float32)
        root_saved = norm_rows(saved_floats)
        scaled_saved = saved_floats * root_saved
        both_normed = jnp.concatenate(
            [(floats * norm_rows(floats)).astype(jnp.bfloat16), scaled_saved.astype(jnp.bfloat16)],
            axis=0,
        )
        pre_both = jnp.dot(both_normed, in_full, preferred_element_type=jnp.float32)
        pre_ahead = pre_both[:length].reshape(1, length, groups, 4, HEAD_DIM)
        pre_back = pre_both[length:].reshape(1, length, groups, 4, HEAD_DIM)
        gated_ahead, unused = heads_forward(pre_ahead, keep_ahead, count_ahead)
        partial_sum = jnp.dot(
            gated_ahead.reshape(length, slab_rows), out_full, preferred_element_type=jnp.float32
        )
        summed = lax.psum(partial_sum.astype(jnp.bfloat16), "cores").astype(jnp.float32)
        outgoing = (floats + summed).astype(jnp.bfloat16)
        ahead_out.append(lax.dynamic_slice_in_dim(outgoing, row_start, share, 0))
        if tick_no + 1 < ticks:
            received = from_behind(outgoing, "section", 1)
        gated_back, saved = heads_forward(pre_back, keep_back, count_back)
        grad_gated = (
            jnp.einsum("sd,fd->sf", upstream, out_full, preferred_element_type=jnp.float32)
            .astype(jnp.bfloat16)
            .reshape(1, length, groups, HEAD_DIM)
        )
        grad_pre = heads_backward(pre_back, saved, grad_gated).reshape(length, columns)
        grad_normed = jnp.einsum("sf,df->sd", grad_pre, in_full, preferred_element_type=jnp.float32)
        back_part = root_saved * (
            grad_normed
            - scaled_saved * jnp.mean(grad_normed * scaled_saved, axis=-1, keepdims=True)
        )
        back_sum = lax.psum(back_part.astype(jnp.bfloat16), "cores").astype(jnp.float32)
        grad_in = (upstream.astype(jnp.float32) + back_sum).astype(jnp.bfloat16)
        back_out.append(lax.dynamic_slice_in_dim(grad_in, row_start, share, 0))
        gated_list.append(gated_back.reshape(length, slab_rows))
        upstream_list.append(upstream)
        if tick_no + 1 < ticks:
            returned = from_behind(grad_in, "section", -1)
    stacked_gated = jnp.concatenate(gated_list, axis=0)
    stacked_upstream = jnp.concatenate(upstream_list, axis=0)
    product = lax.dot_general(
        stacked_gated,
        stacked_upstream,
        (((0,), (0,)), ((), ())),
        preferred_element_type=jnp.float32,
    )
    scaling = (ticks * length * lax.axis_size("dp")) ** (-0.5)
    grads_sum = (
        lax.psum_scatter(
            product.astype(jnp.bfloat16), "dp", scatter_dimension=1, tiled=True
        ).astype(jnp.float32)
        * scaling
    )
    return (jnp.stack(ahead_out)[None], jnp.stack(back_out)[None], grads_sum[None])


def solution(mesh):
    in_specs = (
        P(None, "dp", None),
        P("section", "dp", None),
        P(None, "dp", None),
        P("section", "dp", None),
        P("section", None, "dp", None),
        P("section", "dp", "cores"),
        P("section", "cores", "dp"),
        P("dp", None),
        P("dp", None),
        P("dp", None, None, None),
        P("dp", None, None, None),
    )
    out_specs = (
        P("section", None, ("dp", "cores"), None),
        P("section", None, ("dp", "cores"), None),
        P("section", "cores", "dp"),
    )
    return jax.shard_map(
        per_device, mesh=mesh, in_specs=in_specs, out_specs=out_specs, check_vma=False
    )
```

profile of v0, /device:TPU:8, one launch (start us, length us, event | category | flops | bytes accessed | tf_op | source)
XLA Modules:
  0.0 493.3 jit_solution(5450123814144851031)
XLA Ops:
  8.7 1.4 fusion.137
  14.6 1.4 fusion.78
  18.4 73.2 %all-gather.7.cloned.1.call-done = bf16[1,512,2048]{2,1,0:T(8,128)(2,1)} async-done(((bf16[1,512,128]{2,1,0:T(8,128)(2,1)}), bf16[1,512,2048]{2,1,0:T(8,128)(2,1)}) %all-gather.7.cloned.1.call-update) | async-done | bytes 2097168 | tf_op jit(solution)/shard_map/all_gather | solution.py:130
  91.6 2.4 fusion.31
  94.7 104.7 %all-gather.5.cloned.1.call-done = bf16[1,2048,2048]{2,1,0:T(8,128)(2,1)} async-done(((bf16[1,128,2048]{2,1,0:T(8,128)(2,1)}), bf16[1,2048,2048]{2,1,0:T(8,128)(2,1)}) %all-gather.5.cloned.1.call-update) | async-done | bytes 8388624 | tf_op jit(solution)/shard_map/all_gather | solution.py:135
  199.4 5.2 %fusion.6 = f32[192,2048]{1,0:T(8,128)S(1)} fusion(bf16[1,2048,2048]{2,1,0:T(8,128)(2,1)} %all-gather.5.cloned.1.call-done, bf16[96,2048]{1,0:T(8,128)(2,1)S(1)} %get-tuple-element.54, bf16[96,2048]{1,0:T(8,128)(2,1)S(1)} %get-tuple-element.55), kind=kOutput, calls=%fused_computation.6 | convolution fusion | flops 1612185600 | bytes 10747904 | tf_op jit(solution)/shard_map/dot_general | solution.py:165
  213.5 1.4 pad_maximum_fusion
  215.4 1.2 stack.60
  216.6 6.5 %fusion.68 = (f32[96]{0:T(128)S(1)}, f32[96]{0:T(128)S(1)}, f32[96,2048]{1,0:T(8,128)S(1)}) fusion(f32[96]{0:T(128)S(1)} %add_rsqrt_fusion.6, bf16[1,2,96,2048]{3,2,1,0:T(8,128)(2,1)S(1)} %copy-done.1, bf16[1,2048,2048]{2,1,0:T(8,128)(2,1)} %all-gather.5.cloned.1.call-done, f32[96,2048]{1,0:T(8,128)} %stack.60, f32[192,2048]{1,0:T(8,128)S(1)} %copy-done.10), kind=kOutput, calls=%fused_computation.86 | convolution fusion | flops 808451840 | bytes 11535616 | tf_op jit(solution)/shard_map/sf,df->sd/dot_general | solution.py:184
  225.0 1.2 convolution_convert_fusion.2
  228.6 30.0 %all-reduce.7.cloned.1.call-done = (bf16[96,2048]{1,0:T(8,128)(2,1)}, bf16[96,2048]{1,0:T(8,128)(2,1)}) async-done(((bf16[96,2048]{1,0:T(8,128)(2,1)}, bf16[96,2048]{1,0:T(8,128)(2,1)}), (bf16[96,2048]{1,0:T(8,128)(2,1)}, bf16[96,2048]{1,0:T(8,128)(2,1)})) %all-reduce.7.cloned.1.call-update) | async-done | bytes 786448 | tf_op jit(solution)/shard_map/psum | solution.py:172
  259.8 8.1 %collective-permute-start = (bf16[96,2048]{1,0:T(8,128)(2,1)S(1)}, bf16[96,2048]{1,0:T(8,128)(2,1)S(1)}, u32[]{:S(2)}, u32[]{:S(2)}) collective-permute-start(bf16[96,2048]{1,0:T(8,128)(2,1)S(1)} %fusion.80), channel_id=1, source_target_pairs={{0,32},{32,64},{64,96},{96,128},{128,160},{160,192},{192,224},{224... | collective-permute-start | bytes 1179656 | tf_op jit(solution)/shard_map/ppermute | solution.py:15
  267.9 1.9 add_convert_fusion
  269.8 2.8 collective-permute-start.1
  272.6 26.8 %collective-permute-done = bf16[96,2048]{1,0:T(8,128)(2,1)S(1)} collective-permute-done((bf16[96,2048]{1,0:T(8,128)(2,1)S(1)}, bf16[96,2048]{1,0:T(8,128)(2,1)S(1)}, u32[]{:S(2)}, u32[]{:S(2)}) %collective-permute-start) | collective-permute-done | bytes 393248 | tf_op jit(solution)/shard_map/ppermute | solution.py:15
  299.8 5.2 %fusion.4 = f32[192,2048]{1,0:T(8,128)S(1)} fusion(bf16[1,2048,2048]{2,1,0:T(8,128)(2,1)} %all-gather.5.cloned.1.call-done, bf16[96,2048]{1,0:T(8,128)(2,1)S(1)} %copy-done.21, bf16[96,2048]{1,0:T(8,128)(2,1)S(1)} %multiply_convert_fusion.2), kind=kOutput, calls=%fused_computation.4 | convolution fusion | flops 1612185600 | bytes 10747904 | tf_op jit(solution)/shard_map/dot_general | solution.py:165
  306.2 1.2 fusion.157
  307.5 2.5 reshape.826
  310.0 2.4 fusion.152
  315.3 1.5 fusion.28
  317.8 1.9 multiply_convert_fusion.5
  324.8 2.6 reshape.822
  327.4 2.5 fusion.153
  329.9 2.0 multiply_reduce_fusion.5
  334.9 1.4 copy.67
  336.3 2.4 stack.67
  338.7 6.8 %fusion.73 = (f32[96]{0:T(128)S(1)}, f32[96,2048]{1,0:T(8,128)S(1)}) fusion(f32[96]{0:T(128)S(1)} %add_rsqrt_fusion.4, bf16[1,2,96,2048]{3,2,1,0:T(8,128)(2,1)} %param.15, bf16[1,2048,2048]{2,1,0:T(8,128)(2,1)} %all-gather.5.cloned.1.call-done, f32[96,2048]{1,0:T(8,128)} %stack.67, f32[192,2048]{1,0:T(8,128)} %copy-done.8), kind=kOutput, calls=%fused_computation.91 | convolution fusion | flops 807862144 | bytes 11141888 | tf_op jit(solution)/shard_map/sf,df->sd/dot_general | solution.py:184
  346.5 1.2 convolution_convert_fusion.1
  347.9 1.7 convolution_convert_fusion
  349.7 2.5 copy.74
  354.2 35.7 %all-reduce.5.cloned.1.call-done = (bf16[96,2048]{1,0:T(8,128)(2,1)}, bf16[96,2048]{1,0:T(8,128)(2,1)}) async-done(((bf16[96,2048]{1,0:T(8,128)(2,1)}, bf16[96,2048]{1,0:T(8,128)(2,1)}), (bf16[96,2048]{1,0:T(8,128)(2,1)}, bf16[96,2048]{1,0:T(8,128)(2,1)})) %all-reduce.5.cloned.1.call-update) | async-done | bytes 786448 | tf_op jit(solution)/shard_map/psum | solution.py:172
  393.4 91.7 %reduce-scatter.4.cloned.1.call-done = bf16[128,512]{1,0:T(8,128)(2,1)} async-done(((bf16[2048,512]{1,0:T(8,128)(2,1)}), bf16[128,512]{1,0:T(8,128)(2,1)}) %reduce-scatter.4.cloned.1.call-update) | async-done | bytes 131088
  (148 shorter events, 42.8 us)
Async XLA Ops:
  7.2 11.0 %copy-start.1 = (bf16[1,2,96,2048]{3,2,1,0:T(8,128)(2,1)S(1)}, bf16[1,2,96,2048]{3,2,1,0:T(8,128)(2,1)}, u32[]{:S(2)}) copy-start(bf16[1,2,96,2048]{3,2,1,0:T(8,128)(2,1)} %param.15) | copy-start | bytes 2359300
  7.2 10.9 %copy-start.24 = (bf16[1,96,2048]{2,1,0:T(8,128)(2,1)S(1)}, bf16[1,96,2048]{2,1,0:T(8,128)(2,1)}, u32[]{:S(2)}) copy-start(bf16[1,96,2048]{2,1,0:T(8,128)(2,1)} %param.14) | copy-start | bytes 1179652
  7.2 10.9 %copy-start.17 = (bf16[2,96,2048]{2,1,0:T(8,128)(2,1)S(1)}, bf16[2,96,2048]{2,1,0:T(8,128)(2,1)}, u32[]{:S(2)}) copy-start(bf16[2,96,2048]{2,1,0:T(8,128)(2,1)} %param.13) | copy-start | bytes 2359300
  7.2 84.4 %all-gather.7.cloned.1.call-start = ((), (), s32[]{:S(2)}) async-start(), calls=%async_computation.2 | async-start | bytes 2228224 | tf_op jit(solution)/shard_map/all_gather | solution.py:130
  7.9 191.5 %all-gather.5.cloned.1.call-start = ((), (), s32[]{:S(2)}) async-start(), calls=%async_computation.1 | async-start | bytes 8912896 | tf_op jit(solution)/shard_map/all_gather | solution.py:135
  8.7 249.9 %all-reduce.7.cloned.1.call-start = ((), (), s32[]{:S(2)}) async-start(), calls=%async_computation.5 | async-start | bytes 1572864 | tf_op jit(solution)/shard_map/psum | solution.py:172
  16.0 78.0 %copy-start.5 = (bf16[1,96,2048]{2,1,0:T(8,128)(2,1)}, bf16[1,96,2048]{2,1,0:T(8,128)(2,1)S(1)}, u32[]{:S(2)}) copy-start(bf16[1,96,2048]{2,1,0:T(8,128)(2,1)S(1)} %get-tuple-element.28) | copy-start | bytes 1179652
  204.6 1.1 copy-start.9
  210.4 1.8 copy-start.29
  213.5 3.1 copy-start.10
  223.1 1.9 copy-start
  223.2 1.9 copy-start.19
  224.3 34.3 %copy-start.6 = (bf16[1,96,2048]{2,1,0:T(8,128)(2,1)S(1)}, bf16[1,96,2048]{2,1,0:T(8,128)(2,1)}, u32[]{:S(2)}) copy-start(bf16[1,96,2048]{2,1,0:T(8,128)(2,1)} %copy-done.5) | copy-start | bytes 1179652
  226.3 163.6 %all-reduce.5.cloned.1.call-start = ((), (), s32[]{:S(2)}) async-start(), calls=%async_computation.4 | async-start | bytes 1572864 | tf_op jit(solution)/shard_map/psum | solution.py:172
  228.6 84.0 %copy-start.27 = (f32[96,96]{1,0:T(8,128)}, f32[96,96]{1,0:T(8,128)S(1)}, u32[]{:S(2)}) copy-start(f32[96,96]{1,0:T(8,128)S(1)} %fusion.53) | copy-start | bytes 110596
  258.6 40.8 %copy-start.16 = (bf16[2,96,2048]{2,1,0:T(8,128)(2,1)S(1)}, bf16[2,96,2048]{2,1,0:T(8,128)(2,1)}, u32[]{:S(2)}) copy-start(bf16[2,96,2048]{2,1,0:T(8,128)(2,1)} %param.11) | copy-start | bytes 2359300
  259.8 12.8 %copy-start.13 = (bf16[96,2048]{1,0:T(8,128)(2,1)}, bf16[96,2048]{1,0:T(8,128)(2,1)S(1)}, u32[]{:S(2)}) copy-start(bf16[96,2048]{1,0:T(8,128)(2,1)S(1)} %fusion.80) | copy-start | bytes 1179652
  259.8 40.0 %copy-start.21 = (bf16[96,2048]{1,0:T(8,128)(2,1)S(1)}, bf16[96,2048]{1,0:T(8,128)(2,1)}, u32[]{:S(2)}) copy-start(bf16[96,2048]{1,0:T(8,128)(2,1)} %get-tuple-element.37) | copy-start | bytes 1179652
  259.8 39.6 %collective-permute-start = (bf16[96,2048]{1,0:T(8,128)(2,1)S(1)}, bf16[96,2048]{1,0:T(8,128)(2,1)S(1)}, u32[]{:S(2)}, u32[]{:S(2)}) collective-permute-start(bf16[96,2048]{1,0:T(8,128)(2,1)S(1)} %fusion.80), channel_id=1, source_target_pairs={{0,32},{32,64},{64,96},{96,128},{128,160},{160,192},{192,224},{224... | collective-permute-start | bytes 1179656 | tf_op jit(solution)/shard_map/ppermute | solution.py:15
  269.8 43.7 %collective-permute-start.1 = (bf16[96,2048]{1,0:T(8,128)(2,1)}, bf16[96,2048]{1,0:T(8,128)(2,1)}, u32[]{:S(2)}, u32[]{:S(2)}) collective-permute-start(bf16[96,2048]{1,0:T(8,128)(2,1)} %add_convert_fusion), channel_id=1, source_target_pairs={{32,0},{64,32},{96,64},{128,96},{160,128},{192,160},{224,192},{256... | collective-permute-start | bytes 1179656 | tf_op jit(solution)/shard_map/ppermute | solution.py:15
  305.0 1.2 copy-start.8
  310.0 3.5 copy-start.18
  317.8 4.4 copy-start.12
  317.8 6.1 %copy-start.26 = (f32[4,96,96]{2,1,0:T(8,128)S(1)}, f32[4,96,96]{2,1,0:T(8,128)}, u32[]{:S(2)}) copy-start(f32[4,96,96]{2,1,0:T(8,128)} %copy-done.25) | copy-start | bytes 442372
  317.8 6.1 %copy-start.28 = (f32[96,96]{1,0:T(8,128)S(1)}, f32[96,96]{1,0:T(8,128)}, u32[]{:S(2)}) copy-start(f32[96,96]{1,0:T(8,128)} %copy-done.27) | copy-start | bytes 110596
  327.4 6.3 %copy-start.15 = (f32[1,96,4,1,128]{4,1,2,3,0:T(8,128)S(1)}, f32[1,96,4,1,128]{4,1,2,3,0:T(8,128)}, u32[]{:S(2)}) copy-start(f32[1,96,4,1,128]{4,1,2,3,0:T(8,128)} %get-tuple-element.39) | copy-start | bytes 589828
  338.7 6.8 %copy-start.2 = (bf16[1,2,96,2048]{3,2,1,0:T(8,128)(2,1)S(1)}, bf16[1,2,96,2048]{3,2,1,0:T(8,128)(2,1)}, u32[]{:S(2)}) copy-start(bf16[1,2,96,2048]{3,2,1,0:T(8,128)(2,1)} %param.15) | copy-start | bytes 2359300
  338.7 7.8 %copy-start.20 = (bf16[1,96,4,128]{3,2,1,0:T(4,128)(2,1)S(1)}, bf16[1,96,4,128]{3,2,1,0:T(4,128)(2,1)}, u32[]{:S(2)}) copy-start(bf16[1,96,4,128]{3,2,1,0:T(4,128)(2,1)} %copy.53) | copy-start | bytes 294916
  345.4 2.3 copy-start.22
  346.5 1.4 copy-start.23
  347.7 137.4 %reduce-scatter.4.cloned.1.call-start = ((), (), s32[]{:S(2)}) async-start(), calls=%async_computation.3 | async-start | bytes 2228224
  352.2 38.6 %copy-start.4 = (bf16[96,2048]{1,0:T(8,128)(2,1)S(1)}, bf16[96,2048]{1,0:T(8,128)(2,1)}, u32[]{:S(2)}) copy-start(bf16[96,2048]{1,0:T(8,128)(2,1)} %copy-done.3) | copy-start | bytes 1179652
  (6 other events, 5.6 us)
Sparse Core Ops, SparseCore 0:
  10.0 81.4 all-gather.6
  93.7 105.7 all-gather.4
  226.4 32.1 all-reduce.6
  347.8 42.0 all-reduce.4
  392.6 92.4 reduce-scatter.3
where the time goes:
time: 494 us; the launch traced here: 493 us
  waiting for transfers between devices  364 us (74%)
  matrix products  45.3 us (9%)
  other arithmetic  30.4 us (6%)
  local copies, waits for them, and re-layouts  25.8 us (5%)
  between operations  17.2 us (3%)
  starting transfers between devices  11.1 us (2%)
    all_gather x1, waiting for transfers between devices, per_device(): in_full = lax.all_gather(in_weight[0], 'dp', axis=0, tiled=True)  105 us
    unnamed x6, waiting for transfers between devices  93.1 us
    all_gather x1, waiting for transfers between devices, per_device(): out_full = lax.all_gather(out_weight[0], 'dp', axis=1, tiled=True)  73.2 us
    psum x2, waiting for transfers between devices, per_device(): lax.psum(partial_sum.astype(jnp.bfloat16), 'cores').astype(jnp.float32)  65.7 us
    ppermute x2, waiting for transfers between devices, from_behind(): return lax.ppermute(x, axis, pairs)  26.8 us
    dot_general x2, matrix products, per_device(): jnp.einsum('sf,df->sd', grad_pre, in_full, preferred_element_type=jnp.flo...  13.3 us
    ppermute x2, starting transfers between devices, from_behind(): return lax.ppermute(x, axis, pairs)  10.9 us
    dot_general x2, matrix products, per_device(): pre_both = jnp.dot(both_normed, in_full, preferred_element_type=jnp.float32)  10.4 us
  transfers between devices with their start and end apart: 7, of which 6 were waited for; matrix products, arithmetic and copies ran while one was open for 7% of the time, Pallas kernels for 0%

commit v1 on v0

--- a/solution.py
+++ b/solution.py
@@ -127,7 +127,11 @@
     length = arrivals.shape[1]
     share = length // lax.axis_size("cores")
     row_start = core_no * share
-    out_full = lax.all_gather(out_weight[0], "dp", axis=1, tiled=True)
+    block = out_weight[0]
+    size = lax.axis_size("dp")
+    pieces = jnp.stack([block for _ in range(size)])
+    pieces = lax.all_to_all(pieces, "dp", split_axis=0, concat_axis=0)
+    out_full = jnp.concatenate(pieces, axis=1)
     slab_rows = out_full.shape[0]
     groups = slab_rows // HEAD_DIM
     columns = in_weight.shape[2]

time: 494 us -> 465 us (0.941)
  waiting for transfers between devices: 364 us -> 313 us
  starting transfers between devices: 11.1 us -> 21.1 us
  local copies, waits for them, and re-layouts: 25.8 us -> 32.8 us
    all_to_all x0 -> x1, waiting for transfers between devices: none -> 118 us  [per_device(): pieces = lax.all_to_all(pieces, 'dp', split_axis=0, concat_axis=0)]
    all_gather x1, waiting for transfers between devices: 105 us -> 0.02 us  [per_device(): in_full = lax.all_gather(in_weight[0], 'dp', axis=0, tiled=True)]
    all_gather x1 -> x0, waiting for transfers between devices: 73.2 us -> none  [per_device(): out_full = lax.all_gather(out_weight[0], 'dp', axis=1, tiled=True)]
    psum x2, waiting for transfers between devices: 65.7 us -> 76.1 us  [per_device(): lax.psum(partial_sum.astype(jnp.bfloat16), 'cores').astype(jnp.float32)]
    all_to_all x0 -> x1, starting transfers between devices: none -> 9.97 us  [per_device(): pieces = lax.all_to_all(pieces, 'dp', split_axis=0, concat_axis=0)]
    unnamed x6 -> x5, waiting for transfers between devices: 93.1 us -> 92.4 us
  transfers between devices with their start and end apart: 7 -> 7, of which waited for: 6 -> 5; matrix products, arithmetic and copies ran while one was open for 7% -> 8% of each run, Pallas kernels for 0% -> 0%
where the time goes in v1:
time: 465 us; the launch traced here: 464 us
  waiting for transfers between devices  313 us (67%)
  matrix products  45.6 us (10%)
  other arithmetic  34 us (7%)
  local copies, waits for them, and re-layouts  32.8 us (7%)
  starting transfers between devices  21.1 us (5%)
  between operations  17.1 us (4%)
    all_to_all x1, waiting for transfers between devices, per_device(): pieces = lax.all_to_all(pieces, 'dp', split_axis=0, concat_axis=0)  118 us
    unnamed x5, waiting for transfers between devices  92.4 us
    psum x2, waiting for transfers between devices, per_device(): lax.psum(partial_sum.astype(jnp.bfloat16), 'cores').astype(jnp.float32)  76.1 us
    ppermute x2, waiting for transfers between devices, from_behind(): return lax.ppermute(x, axis, pairs)  26.8 us
    dot_general x2, matrix products, per_device(): jnp.einsum('sf,df->sd', grad_pre, in_full, preferred_element_type=jnp.flo...  13.2 us
    ppermute x2, starting transfers between devices, from_behind(): return lax.ppermute(x, axis, pairs)  11 us
    dot_general x2, matrix products, per_device(): pre_both = jnp.dot(both_normed, in_full, preferred_element_type=jnp.float32)  10.6 us
    another operation x6, other arithmetic  10.1 us
  transfers between devices with their start and end apart: 7, of which 5 were waited for; matrix products, arithmetic and copies ran while one was open for 8% of the time, Pallas kernels for 0%

profile of v1, /device:TPU:8, one launch (start us, length us, event | category | flops | bytes accessed | tf_op | source)
XLA Modules:
  0.0 463.6 jit_solution(12981092719714051457)
XLA Ops:
  8.9 1.6 stack.55
  10.5 10.0 %all-to-all-start = ((bf16[16,512,128]{1,2,0:T(8,128)(2,1)}), bf16[16,512,128]{1,2,0:T(8,128)(2,1)S(1)}, u32[]{:S(2)}, u32[]{:S(2)}) async-start(bf16[16,512,128]{1,2,0:T(8,128)(2,1)} %stack.55), calls=%async_computation | async-start | bytes 4194304 | tf_op jit(solution)/shard_map/all_to_all | solution.py:133
  23.3 2.0 fusion.62
  28.0 2.1 fusion.51
  30.1 117.6 %all-to-all-done = bf16[16,512,128]{1,2,0:T(8,128)(2,1)S(1)} async-done(((bf16[16,512,128]{1,2,0:T(8,128)(2,1)}), bf16[16,512,128]{1,2,0:T(8,128)(2,1)S(1)}, u32[]{:S(2)}, u32[]{:S(2)}) %all-to-all-start) | async-done | bytes 2097184 | tf_op jit(solution)/shard_map/all_to_all | solution.py:133
  149.9 5.4 %fusion.6 = f32[192,2048]{1,0:T(8,128)S(1)} fusion(bf16[1,2048,2048]{2,1,0:T(8,128)(2,1)} %all-gather.3.cloned.1.call-done, bf16[96,2048]{1,0:T(8,128)(2,1)} %get-tuple-element.54, bf16[96,2048]{1,0:T(8,128)(2,1)} %get-tuple-element.55), kind=kOutput, calls=%fused_computation.6 | convolution fusion | flops 1612185600 | bytes 10747904 | tf_op jit(solution)/shard_map/dot_general | solution.py:169
  157.8 2.5 reshape.834
  160.4 1.5 fusion.139
  166.3 2.6 reshape.828
  168.8 2.5 fusion.140
  171.3 2.0 multiply_reduce_fusion.6
  174.6 1.5 convolution_convert_fusion.2
  177.6 2.4 stack.64
  179.9 6.8 %fusion.52 = (f32[96]{0:T(128)S(1)}, f32[96]{0:T(128)S(1)}, f32[96,2048]{1,0:T(8,128)S(1)}) fusion(f32[96]{0:T(128)S(1)} %add_rsqrt_fusion.6, bf16[1,2,96,2048]{3,2,1,0:T(8,128)(2,1)S(1)} %copy-done, bf16[1,2048,2048]{2,1,0:T(8,128)(2,1)} %all-gather.3.cloned.1.call-done, f32[96,2048]{1,0:T(8,128)} %stack.64, f32[192,2048]{1,0:T(8,128)} %copy-done.5), kind=kOutput, calls=%fused_computation.80 | convolution fusion | flops 808451840 | bytes 11535488 | tf_op jit(solution)/shard_map/sf,df->sd/dot_general | solution.py:188
  190.2 40.4 %all-reduce.7.cloned.1.call-done = (bf16[96,2048]{1,0:T(8,128)(2,1)}, bf16[96,2048]{1,0:T(8,128)(2,1)}) async-done(((bf16[96,2048]{1,0:T(8,128)(2,1)}, bf16[96,2048]{1,0:T(8,128)(2,1)}), (bf16[96,2048]{1,0:T(8,128)(2,1)}, bf16[96,2048]{1,0:T(8,128)(2,1)})) %all-reduce.7.cloned.1.call-update) | async-done | bytes 786448 | tf_op jit(solution)/shard_map/psum | solution.py:176
  231.9 8.1 %collective-permute-start = (bf16[96,2048]{1,0:T(8,128)(2,1)S(1)}, bf16[96,2048]{1,0:T(8,128)(2,1)S(1)}, u32[]{:S(2)}, u32[]{:S(2)}) collective-permute-start(bf16[96,2048]{1,0:T(8,128)(2,1)S(1)} %fusion.64), channel_id=1, source_target_pairs={{0,32},{32,64},{64,96},{96,128},{128,160},{160,192},{192,224},{224... | collective-permute-start | bytes 1179656 | tf_op jit(solution)/shard_map/ppermute | solution.py:15
  240.0 1.8 add_convert_fusion
  241.9 2.8 collective-permute-start.1
  244.7 26.8 %collective-permute-done = bf16[96,2048]{1,0:T(8,128)(2,1)S(1)} collective-permute-done((bf16[96,2048]{1,0:T(8,128)(2,1)S(1)}, bf16[96,2048]{1,0:T(8,128)(2,1)S(1)}, u32[]{:S(2)}, u32[]{:S(2)}) %collective-permute-start) | collective-permute-done | bytes 393248 | tf_op jit(solution)/shard_map/ppermute | solution.py:15
  272.9 5.2 %fusion.4 = f32[192,2048]{1,0:T(8,128)S(1)} fusion(bf16[1,2048,2048]{2,1,0:T(8,128)(2,1)} %all-gather.3.cloned.1.call-done, bf16[96,2048]{1,0:T(8,128)(2,1)S(1)} %copy-done.17, bf16[96,2048]{1,0:T(8,128)(2,1)S(1)} %multiply_convert_fusion.2), kind=kOutput, calls=%fused_computation.4 | convolution fusion | flops 1612185600 | bytes 10747904 | tf_op jit(solution)/shard_map/dot_general | solution.py:169
  280.5 2.5 reshape.836
  283.1 2.4 fusion.136
  290.6 1.9 multiply_convert_fusion.5
  297.6 2.6 reshape.832
  300.1 2.5 fusion.137
  302.6 2.0 multiply_reduce_fusion.5
  305.9 1.5 convolution_convert_fusion.1
  310.4 6.5 %fusion.57 = (f32[96]{0:T(128)S(1)}, f32[96,2048]{1,0:T(8,128)S(1)}) fusion(f32[96]{0:T(128)S(1)} %add_rsqrt_fusion.4, bf16[1,2,96,2048]{3,2,1,0:T(8,128)(2,1)S(1)} %copy-done.1, bf16[1,2048,2048]{2,1,0:T(8,128)(2,1)} %all-gather.3.cloned.1.call-done, f32[96,2048]{1,0:T(8,128)S(1)} %stack.71, f32[192,2048]{1,0:T(8,128)} %copy-done.4), kind=kOutput, calls=%fused_computation.85 | convolution fusion | flops 807862144 | bytes 11141888 | tf_op jit(solution)/shard_map/sf,df->sd/dot_general | solution.py:188
  318.2 1.7 convolution_convert_fusion
  319.9 2.5 copy.76
  324.4 35.7 %all-reduce.5.cloned.1.call-done = (bf16[96,2048]{1,0:T(8,128)(2,1)}, bf16[96,2048]{1,0:T(8,128)(2,1)}) async-done(((bf16[96,2048]{1,0:T(8,128)(2,1)}, bf16[96,2048]{1,0:T(8,128)(2,1)}), (bf16[96,2048]{1,0:T(8,128)(2,1)}, bf16[96,2048]{1,0:T(8,128)(2,1)})) %all-reduce.5.cloned.1.call-update) | async-done | bytes 786448 | tf_op jit(solution)/shard_map/psum | solution.py:176
  363.6 91.6 %reduce-scatter.4.cloned.1.call-done = bf16[128,512]{1,0:T(8,128)(2,1)} async-done(((bf16[2048,512]{1,0:T(8,128)(2,1)}), bf16[128,512]{1,0:T(8,128)(2,1)}) %reduce-scatter.4.cloned.1.call-update) | async-done | bytes 131088
  (151 shorter events, 47.4 us)
Async XLA Ops:
  7.2 142.7 %all-gather.3.cloned.1.call-start = ((), (), s32[]{:S(2)}) async-start(), calls=%async_computation.2 | async-start | bytes 8912896 | tf_op jit(solution)/shard_map/all_gather | solution.py:139
  10.5 10.1 %copy-start.27 = (s32[1,17]{1,0:T(1,128)S(1)}, s32[1,17]{1,0:T(1,128)}, u32[]{:S(2)}) copy-start(s32[1,17]{1,0:T(1,128)} %param.19) | copy-start | bytes 208
  10.5 10.1 %copy-start.28 = (s32[1,17]{1,0:T(1,128)S(1)}, s32[1,17]{1,0:T(1,128)}, u32[]{:S(2)}) copy-start(s32[1,17]{1,0:T(1,128)} %param.18) | copy-start | bytes 208
  10.5 12.2 %copy-start.25 = (s32[1,17,4,4]{1,3,2,0:T(4,128)S(1)}, s32[1,17,4,4]{1,3,2,0:T(4,128)}, u32[]{:S(2)}) copy-start(s32[1,17,4,4]{1,3,2,0:T(4,128)} %param.20) | copy-start | bytes 3268
  10.5 12.5 %copy-start.26 = (s32[1,17,4,4]{1,3,2,0:T(4,128)S(1)}, s32[1,17,4,4]{1,3,2,0:T(4,128)}, u32[]{:S(2)}) copy-start(s32[1,17,4,4]{1,3,2,0:T(4,128)} %param.21) | copy-start | bytes 3268
  10.5 12.7 %copy-start = (bf16[1,2,96,2048]{3,2,1,0:T(8,128)(2,1)S(1)}, bf16[1,2,96,2048]{3,2,1,0:T(8,128)(2,1)}, u32[]{:S(2)}) copy-start(bf16[1,2,96,2048]{3,2,1,0:T(8,128)(2,1)} %param.15) | copy-start | bytes 2359300
  10.5 12.8 %copy-start.20 = (bf16[1,96,2048]{2,1,0:T(8,128)(2,1)S(1)}, bf16[1,96,2048]{2,1,0:T(8,128)(2,1)}, u32[]{:S(2)}) copy-start(bf16[1,96,2048]{2,1,0:T(8,128)(2,1)} %param.12) | copy-start | bytes 1179652
  10.5 137.2 %all-to-all-start = ((bf16[16,512,128]{1,2,0:T(8,128)(2,1)}), bf16[16,512,128]{1,2,0:T(8,128)(2,1)S(1)}, u32[]{:S(2)}, u32[]{:S(2)}) async-start(bf16[16,512,128]{1,2,0:T(8,128)(2,1)} %stack.55), calls=%async_computation | async-start | bytes 4194304 | tf_op jit(solution)/shard_map/all_to_all | solution.py:133
  20.5 210.1 %all-reduce.7.cloned.1.call-start = ((), (), s32[]{:S(2)}) async-start(), calls=%async_computation.5 | async-start | bytes 1572864 | tf_op jit(solution)/shard_map/psum | solution.py:176
  155.3 1.2 copy-start.5
  160.4 1.7 copy-start.31
  171.3 4.8 %copy-start.11 = (f32[1,96,4,1,128]{4,1,2,3,0:T(8,128)S(1)}, f32[1,96,4,1,128]{4,1,2,3,0:T(8,128)}, u32[]{:S(2)}) copy-start(f32[1,96,4,1,128]{4,1,2,3,0:T(8,128)} %get-tuple-element.40) | copy-start | bytes 589828
  173.3 2.8 copy-start.14
  173.3 2.8 copy-start.15
  173.3 2.8 copy-start.22
  188.0 172.1 %all-reduce.5.cloned.1.call-start = ((), (), s32[]{:S(2)}) async-start(), calls=%async_computation.4 | async-start | bytes 1572864 | tf_op jit(solution)/shard_map/psum | solution.py:176
  190.2 95.5 %copy-start.29 = (f32[96,96]{1,0:T(8,128)}, f32[96,96]{1,0:T(8,128)S(1)}, u32[]{:S(2)}) copy-start(f32[96,96]{1,0:T(8,128)S(1)} %fusion.37) | copy-start | bytes 110596
  231.8 12.8 %copy-start.8 = (bf16[96,2048]{1,0:T(8,128)(2,1)}, bf16[96,2048]{1,0:T(8,128)(2,1)S(1)}, u32[]{:S(2)}) copy-start(bf16[96,2048]{1,0:T(8,128)(2,1)S(1)} %fusion.64) | copy-start | bytes 1179652
  231.8 41.0 %copy-start.17 = (bf16[96,2048]{1,0:T(8,128)(2,1)S(1)}, bf16[96,2048]{1,0:T(8,128)(2,1)}, u32[]{:S(2)}) copy-start(bf16[96,2048]{1,0:T(8,128)(2,1)} %get-tuple-element.37) | copy-start | bytes 1179652
  231.9 39.6 %collective-permute-start = (bf16[96,2048]{1,0:T(8,128)(2,1)S(1)}, bf16[96,2048]{1,0:T(8,128)(2,1)S(1)}, u32[]{:S(2)}, u32[]{:S(2)}) collective-permute-start(bf16[96,2048]{1,0:T(8,128)(2,1)S(1)} %fusion.64), channel_id=1, source_target_pairs={{0,32},{32,64},{64,96},{96,128},{128,160},{160,192},{192,224},{224... | collective-permute-start | bytes 1179656 | tf_op jit(solution)/shard_map/ppermute | solution.py:15
  241.9 44.7 %collective-permute-start.1 = (bf16[96,2048]{1,0:T(8,128)(2,1)}, bf16[96,2048]{1,0:T(8,128)(2,1)}, u32[]{:S(2)}, u32[]{:S(2)}) collective-permute-start(bf16[96,2048]{1,0:T(8,128)(2,1)} %add_convert_fusion), channel_id=1, source_target_pairs={{32,0},{64,32},{96,64},{128,96},{160,128},{192,160},{224,192},{256... | collective-permute-start | bytes 1179656 | tf_op jit(solution)/shard_map/ppermute | solution.py:15
  283.1 3.5 copy-start.16
  290.5 4.4 copy-start.7
  290.6 6.1 %copy-start.24 = (f32[4,96,96]{2,1,0:T(8,128)S(1)}, f32[4,96,96]{2,1,0:T(8,128)}, u32[]{:S(2)}) copy-start(f32[4,96,96]{2,1,0:T(8,128)} %copy-done.23) | copy-start | bytes 442372
  290.6 6.1 %copy-start.30 = (f32[96,96]{1,0:T(8,128)S(1)}, f32[96,96]{1,0:T(8,128)}, u32[]{:S(2)}) copy-start(f32[96,96]{1,0:T(8,128)} %copy-done.29) | copy-start | bytes 110596
  302.6 4.8 %copy-start.10 = (f32[1,96,4,1,128]{4,1,2,3,0:T(8,128)S(1)}, f32[1,96,4,1,128]{4,1,2,3,0:T(8,128)}, u32[]{:S(2)}) copy-start(f32[1,96,4,1,128]{4,1,2,3,0:T(8,128)} %get-tuple-element.39) | copy-start | bytes 589828
  304.6 2.8 copy-start.12
  304.6 2.8 copy-start.13
  304.6 2.8 copy-start.21
  307.4 2.9 copy-start.1
  317.9 137.3 %reduce-scatter.4.cloned.1.call-start = ((), (), s32[]{:S(2)}) async-start(), calls=%async_computation.3 | async-start | bytes 2228224
  322.4 38.6 %copy-start.3 = (bf16[96,2048]{1,0:T(8,128)(2,1)S(1)}, bf16[96,2048]{1,0:T(8,128)(2,1)}, u32[]{:S(2)}) copy-start(bf16[96,2048]{1,0:T(8,128)(2,1)} %copy-done.2) | copy-start | bytes 1179652
  (7 other events, 7.2 us)
Sparse Core Ops, SparseCore 0:
  10.1 135.6 all-gather.2
  188.1 42.4 all-reduce.6
  318.0 42.0 all-reduce.4
  362.8 92.4 reduce-scatter.3
